TPU v7x, 32 devices: a whole 2x2x4 slice. The times are simulated.
32 devices in a mesh: parts: 1, layer: 2 (over core), width: 16 (over z, y, x).
Axes of the slice: x: 2, y: 2, z: 4, core: 2. Of those that a mesh axis runs over, the one named last changes fastest.
Arguments:
- src_ids: int32 [2, 8192, 128], P('layer', ('parts', 'width')), may hold values from 0 to 1023, as said below
- src_acts: bfloat16 [2, 8192, 128], P('layer', ('parts', 'width')), may hold values from 0.099609375 to 4
- tgt_ids: int32 [2, 8192, 128], P(None, ('parts', 'width')), may hold values from 0 to 1023, as said below
- tgt_acts: bfloat16 [2, 8192, 128], P(None, ('parts', 'width')), may hold values from 0.099609375 to 4
- enc_cols: bfloat16 [2, 1024, 4608], P('layer', None, 'width'), may hold values from -0.09375 to 0.09375
- dec_rows: bfloat16 [2, 2, 1024, 4608], P('layer', None, None, 'width'), may hold values from -6 to 6
Outputs:
- edges: float32 [2, 2, 1024, 1024], P(('parts', 'layer'), None, 'width')
Inputs may be any that keep to these rules, and one draw needn't show every extreme that they name: `src_ids`: each token's 64 slots are distinct. `tgt_ids`: each token's 64 slots are distinct.
All inputs are finite; a program needn't handle non-finite values.
Results may differ from a plain program's by a relative error of at most 0.0003.
Values may be sent and summed in bfloat16 or wider, within the bound.
A program may use at most 128 MiB of HBM per device.

v0:
```python
import math

import jax
import jax.numpy as jnp
from jax import lax
from jax.sharding import PartitionSpec as P


def partner(value, axis, bit):
    mask = 2**bit
    pairs = [(source, source ^ mask) for source in range(lax.axis_size(axis))]
    return lax.ppermute(value, axis, pairs)


def dense_acts(ids, acts, count):
    flat_ids = ids.reshape(ids.shape[0] * 2, ids.shape[1] // 2)
    flat_acts = acts.reshape(acts.shape[0] * 2, acts.shape[1] // 2)
    total_rows = flat_ids.shape[0]
    top_count = flat_ids.shape[1]
    block_rows = math.gcd(total_rows, 64)
    blocks = total_rows // block_rows
    id_blocks = flat_ids.reshape(blocks, block_rows, top_count)
    act_blocks = flat_acts.reshape(blocks, block_rows, top_count)
    columns = jnp.arange(count, dtype=jnp.int32)[None, None, :]

    def one_block(pair):
        block_ids, block_acts = pair
        hits = block_ids[:, :, None] == columns
        values = jnp.where(hits, block_acts.astype(jnp.float32)[:, :, None], 0.0)
        return jnp.sum(values, axis=1).astype(jnp.bfloat16)

    dense = lax.map(one_block, (id_blocks, act_blocks))
    return dense.reshape(total_rows, count)


def on_device(src_ids, src_acts, tgt_ids, tgt_acts, enc_cols, dec_rows):
    group = lax.axis_index("layer")
    other = 1 - group
    act_count = enc_cols.shape[1]
    top_count = src_ids.shape[2] // 2
    tok_dev = src_ids.shape[1] * 2
    factor = (act_count / top_count) ** 2 / (tok_dev * lax.axis_size("width"))
    own_enc = enc_cols[0]
    far_enc = partner(own_enc, "layer", 0)
    source = dense_acts(src_ids[0], src_acts[0], act_count)
    tgt_here = dense_acts(
        lax.dynamic_index_in_dim(tgt_ids, group, 0, False),
        lax.dynamic_index_in_dim(tgt_acts, group, 0, False),
        act_count,
    )
    tgt_far = dense_acts(
        lax.dynamic_index_in_dim(tgt_ids, other, 0, False),
        lax.dynamic_index_in_dim(tgt_acts, other, 0, False),
        act_count,
    )
    dec_here = lax.dynamic_index_in_dim(dec_rows[0], group, 0, False)
    dec_far = lax.dynamic_index_in_dim(dec_rows[0], other, 0, False)

    def co_term(target):
        return lax.dot_general(
            source, target, (((0,), (0,)), ((), ())), preferred_element_type=jnp.float32
        )

    def virt_term(decoder, encoder):
        return lax.dot_general(
            decoder, encoder, (((1,), (1,)), ((), ())), preferred_element_type=jnp.float32
        )

    def one_round(decoder, encoder, target):
        summed = lax.psum_scatter(
            jnp.concatenate([virt_term(decoder, encoder), co_term(target)], axis=1),
            "width",
            scatter_dimension=0,
            tiled=True,
        )
        return (summed[:, :act_count], summed[:, act_count:])

    virt_here, co_here = one_round(dec_here, own_enc, tgt_here)
    virt_far, co_far = one_round(dec_far, far_enc, tgt_far)
    edge_here = virt_here * (co_here * factor)
    edge_far = virt_far * (co_far * factor)
    first = jnp.where(group == 0, edge_here, edge_far)
    second = jnp.where(group == 0, edge_far, edge_here)
    return jnp.stack([first, second])[None]


def solution(mesh):
    placed = (
        P("layer", ("parts", "width"), None),
        P("layer", ("parts", "width"), None),
        P(None, ("parts", "width"), None),
        P(None, ("parts", "width"), None),
        P("layer", None, "width"),
        P("layer", None, None, "width"),
    )
    return jax.shard_map(
        on_device,
        mesh=mesh,
        in_specs=placed,
        out_specs=P(("parts", "layer"), None, "width", None),
        check_vma=False,
    )
```

profile of v0, /device:TPU:0, one launch (start us, length us, event | category | flops | bytes accessed | tf_op | source)
XLA Modules:
  0.0 573.8 jit_solution(12757020726713790721)
XLA Ops:
  14.3 76.6 %while.33 = (s32[]{:T(128)}, bf16[16,64,1024]{2,1,0:T(8,128)(2,1)S(1)}, s32[16,64,64]{2,1,0:T(8,128)}, bf16[16,64,64]{2,1,0:T(8,128)(2,1)}, s32[]{:T(128)}) while((s32[]{:T(128)}, bf16[16,64,1024]{2,1,0:T(8,128)(2,1)S(1)}, s32[16,64,64]{2,1,0:T(8,128)}, bf16[16,64,64]{2,1,0:T(8,128)(2,1)}, s32[]{:T(128)}) %tuple.58), condition=%wide.region_2.3_spmd.clone, body=%wide.region_0.2_spmd.clone.sunk | while | flops 12521474 | bytes 483401 | solution.py:32
  39.8 3.3 select_reduce_fusion.6
  44.6 3.3 select_reduce_fusion.6
  49.4 3.3 select_reduce_fusion.6
  54.1 3.3 select_reduce_fusion.6
  58.9 3.3 select_reduce_fusion.6
  82.9 3.3 select_reduce_fusion.6
  87.6 3.3 select_reduce_fusion.6
  96.4 86.6 %while.34 = (s32[]{:T(128)}, bf16[16,64,1024]{2,1,0:T(8,128)(2,1)}, s32[16,64,64]{2,1,0:T(8,128)}, bf16[16,64,64]{2,1,0:T(8,128)(2,1)}, s32[]{:T(128)}) while((s32[]{:T(128)}, bf16[16,64,1024]{2,1,0:T(8,128)(2,1)}, s32[16,64,64]{2,1,0:T(8,128)}, bf16[16,64,64]{2,1,0:T(8,128)(2,1)}, s32[]{:T(128)}) %tuple.61), condition=%wide.region_5.6_spmd.clone, body=%wide.region_3.5_spmd.clone.sunk | while | flops 12521474 | bytes 483909 | solution.py:32
  114.1 3.3 select_reduce_fusion.7
  124.9 3.3 select_reduce_fusion.7
  130.3 3.3 select_reduce_fusion.7
  135.7 3.3 select_reduce_fusion.7
  146.6 3.3 select_reduce_fusion.7
  152.0 3.3 select_reduce_fusion.7
  157.4 3.3 select_reduce_fusion.7
  173.6 3.3 select_reduce_fusion.7
  187.9 4.1 pad_maximum_fusion
  192.0 9.2 %copy.10 = f32[1024,2048]{1,0:T(8,128)} copy(f32[1024,2048]{0,1:T(8,128)} %pad_maximum_fusion) | data formatting | bytes 16777216
  202.8 65.4 %while.35 = (s32[]{:T(128)}, bf16[16,64,1024]{2,1,0:T(8,128)(2,1)S(1)}, s32[16,64,64]{2,1,0:T(8,128)}, bf16[16,64,64]{2,1,0:T(8,128)(2,1)S(1)}, s32[]{:T(128)}) while((s32[]{:T(128)}, bf16[16,64,1024]{2,1,0:T(8,128)(2,1)S(1)}, s32[16,64,64]{2,1,0:T(8,128)}, bf16[16,64,64]{2,1,0:T(8,128)(2,1)S(1)}, s32[]{:T(128)}) %tuple.64), condition=%wide.region_9.10_spmd.clone, body=%wide.region_7.9_spmd.clone.sunk | while | flops 12521474 | bytes 483401 | solution.py:32
  203.6 3.3 select_reduce_fusion.8
  211.8 3.3 select_reduce_fusion.8
  224.1 3.3 select_reduce_fusion.8
  232.2 3.3 select_reduce_fusion.8
  236.3 3.3 select_reduce_fusion.8
  248.6 3.3 select_reduce_fusion.8
  252.7 3.3 select_reduce_fusion.8
  268.2 4.0 convolution_bitcast_fusion
  274.6 4.1 pad_maximum_fusion.1
  278.7 9.2 %copy.12 = f32[1024,2048]{1,0:T(8,128)} copy(f32[1024,2048]{0,1:T(8,128)} %pad_maximum_fusion.1) | data formatting | bytes 16777216
  287.9 93.7 %reduce-scatter.7.cloned.1.call-done = f32[64,2048]{1,0:T(8,128)} async-done(((f32[1024,2048]{1,0:T(8,128)}), f32[64,2048]{1,0:T(8,128)}) %reduce-scatter.7.cloned.1.call-update) | async-done | bytes 524304
  383.1 181.1 %reduce-scatter.9.cloned.1.call-done = f32[64,2048]{1,0:T(8,128)} async-done(((f32[1024,2048]{1,0:T(8,128)}), f32[64,2048]{1,0:T(8,128)}) %reduce-scatter.9.cloned.1.call-update) | async-done | bytes 524304
  (207 shorter events, 182.0 us)
Async XLA Ops:
  6.5 176.4 %copy-start = (bf16[1,2,1024,288]{2,3,1,0:T(8,128)(2,1)S(1)}, bf16[1,2,1024,288]{2,3,1,0:T(8,128)(2,1)}, u32[]{:S(2)}) copy-start(bf16[1,2,1024,288]{2,3,1,0:T(8,128)(2,1)} %param.17) | copy-start | bytes 3538948
  6.5 375.1 %reduce-scatter.7.cloned.1.call-start = ((), (), s32[]{:S(2)}) async-start(), calls=%async_computation.2 | async-start | bytes 8912896
  6.5 265.7 %collective-permute-start = (bf16[1024,288]{0,1:T(8,128)(2,1)}, bf16[1024,288]{0,1:T(8,128)(2,1)}, u32[]{:S(2)}, u32[]{:S(2)}) collective-permute-start(bf16[1024,288]{0,1:T(8,128)(2,1)} %bitcast.65), channel_id=1, source_target_pairs={{0,16},{16,0},{1,17},{17,1},{2,18},{18,2},{3,19},{19,3},{4,20},{20... | collective-permute-start | bytes 1769480 | tf_op jit(solution)/shard_map/ppermute | solution.py:12
  90.9 94.5 %copy-start.1 = (bf16[16,64,1024]{2,1,0:T(8,128)(2,1)}, bf16[16,64,1024]{2,1,0:T(8,128)(2,1)S(1)}, u32[]{:S(2)}) copy-start(bf16[16,64,1024]{2,1,0:T(8,128)(2,1)S(1)} %get-tuple-element.86) | copy-start | bytes 6291460
  183.0 2.5 copy-start.2
  201.2 1.2 copy-start.3
  201.3 363.0 %reduce-scatter.9.cloned.1.call-start = ((), (), s32[]{:S(2)}) async-start(), calls=%async_computation.3 | async-start | bytes 8912896
Sparse Core Ops, SparseCore 0:
  201.4 180.2 reduce-scatter.6
  383.9 180.2 reduce-scatter.8
where the time goes:
time: 581 us; the launch traced here: 574 us
  waiting for transfers between devices  275 us (47%)
  other arithmetic  188 us (32%)
  local copies, waits for them, and re-layouts  84.4 us (15%)
  between operations  13.6 us (2%)
  matrix products  11.3 us (2%)
    unnamed x4, waiting for transfers between devices  275 us
    reduce_sum x48, other arithmetic, one_block(): return jnp.sum(values, axis=1).astype(jnp.bfloat16)  156 us
    eq x48, local copies, waits for them, and re-layouts, one_block(): hits = block_ids[:, :, None] == columns  36.6 us
    convert_element_type x48, other arithmetic, one_block(): values = jnp.where(hits, block_acts.astype(jnp.float32)[:, :, None], 0.0)  23.3 us
    unnamed x14, local copies, waits for them, and re-layouts  19.2 us
  transfers between devices with their start and end apart: 3, of which 2 were waited for; matrix products, arithmetic and copies ran while one was open for 49% of the time, Pallas kernels for 0%

commit v1 on v0

v1 whole, which is shorter than its diff:
```python
import functools

import jax
import jax.numpy as jnp
from jax import lax
from jax.experimental import pallas as pl
from jax.experimental.pallas import tpu as pltpu
from jax.sharding import PartitionSpec as P

MESH = pl.DeviceIdType.MESH
F32 = jnp.float32
BF16 = jnp.bfloat16
QUAD = 4
LANES = 128
UNROLL = 16


def build_dense(ids_ref, acts_ref, lo_s, key_s, act_s, tmp, put, high):
    rows, wide = ids_ref.shape
    per = QUAD * high
    ids = ids_ref[...].astype(jnp.int32)
    token = lax.broadcasted_iota(jnp.int32, ids.shape, 1) // (wide // QUAD)
    lo_s[...] = (ids % LANES).astype(F32)
    key_s[...] = (token * high + ids // LANES).astype(F32)
    act_s[...] = acts_ref[...].astype(F32)
    sub = lax.broadcasted_iota(jnp.int32, (16, wide), 0).astype(F32)

    def one(r):
        def row(ref):
            return jnp.broadcast_to(ref[pl.ds(r, 1), :], (16, wide)).astype(BF16)

        lo, key, act = row(lo_s), row(key_s), row(act_s)
        zero = jnp.zeros((16, wide), BF16)
        ones = jnp.ones((16, wide), BF16)
        b = jnp.concatenate(
            [jnp.where(lo == (sub + 16 * i).astype(BF16), ones, zero) for i in range(LANES // 16)], 0
        )
        a = jnp.concatenate(
            [jnp.where(key == (sub + 16 * i).astype(BF16), act, zero) for i in range(per // 16)], 0
        )
        out = lax.dot_general(a, b, (((1,), (1,)), ((), ())), preferred_element_type=F32)
        tmp[pl.ds(pl.multiple_of(r * per, per), per), :] = out

    def many(g, carry):
        for i in range(UNROLL):
            one(g * UNROLL + i)
        return carry

    lax.fori_loop(0, rows // UNROLL, many, 0)
    for j in range(QUAD):
        for h in range(high):
            put(j, h, tmp[pl.ds(j * high + h, rows, stride=per), :])


def kernel(
    groups, factor,
    sid_ref, sact_ref, tid_ref, tact_ref, enc_ref, dec_ref,
    out_ref,
    tid_g, tact_g, enc_own, enc_far, dec_g, src_out, src_g, tgt_own, tgt_far,
    part, arrived, lo_s, key_s, act_s, tmp,
    tid_ss, tid_rs, tact_ss, tact_rs, enc_ss, enc_rs, dec_ss, dec_rs, src_ss, src_rs,
    fe_ss, fe_rs, ft_ss, ft_rs, z_ss, z_rs,
):
    layer = lax.axis_index("layer")
    width = lax.axis_index("width")
    group, place = width // QUAD, width % QUAD
    rows = tid_ref.shape[0]
    count = enc_ref.shape[1]
    high = count // LANES
    share = count // QUAD
    block = share // groups
    pair = {"layer": 1 - layer}

    def xor(k):
        low, up = place % 2, place // 2
        low = low + (k % 2) * (1 - 2 * low)
        up = up + (k // 2) * (1 - 2 * up)
        return up * 2 + low

    peers = [xor(k) for k in range(QUAD)]
    ids = [{"width": group * QUAD + peers[k]} for k in range(QUAD)]
    ring = [lax.rem(group + s, groups) for s in range(groups)]
    ring_ids = [{"width": ring[s] * QUAD + place} for s in range(groups)]

    def remote(src, dst, ss, rs, to):
        return pltpu.make_async_remote_copy(
            src_ref=src, dst_ref=dst, send_sem=ss, recv_sem=rs, device_id=to, device_id_type=MESH
        )

    barrier = pltpu.get_barrier_semaphore()
    others = ids[1:] + ring_ids[1:] + [pair]
    for to in others:
        pl.semaphore_signal(barrier, inc=1, device_id=to, device_id_type=MESH)
    pl.semaphore_wait(barrier, len(others))

    tids = [remote(tid_ref, tid_g.at[k - 1], tid_ss.at[k - 1], tid_rs.at[k - 1], ids[k]) for k in range(1, QUAD)]
    tacts = [remote(tact_ref, tact_g.at[k - 1], tact_ss.at[k - 1], tact_rs.at[k - 1], ids[k]) for k in range(1, QUAD)]
    decs = [remote(dec_ref.at[peers[k]], dec_g.at[k], dec_ss.at[k - 1], dec_rs.at[k - 1], ids[k]) for k in range(1, QUAD)]
    encs = [remote(enc_ref, enc_own.at[k], enc_ss.at[k - 1], enc_rs.at[k - 1], ids[k]) for k in range(1, QUAD)]
    srcs = [remote(src_out.at[peers[k]], src_g.at[k - 1], src_ss.at[k - 1], src_rs.at[k - 1], ids[k]) for k in range(1, QUAD)]
    far_encs = [remote(enc_ref if k == 0 else enc_own.at[k], enc_far.at[k], fe_ss.at[k], fe_rs.at[k], pair) for k in range(QUAD)]
    far_tgts = [remote(tgt_own.at[k], tgt_far.at[k], ft_ss.at[k], ft_rs.at[k], pair) for k in range(QUAD)]
    sums = [
        [
            remote(
                part.at[i, pl.ds(pl.multiple_of(ring[s] * block, block), block), :],
                arrived.at[s - 1, i], z_ss.at[i, s - 1], z_rs.at[i, s - 1], ring_ids[s],
            )
            for s in range(1, groups)
        ]
        for i in range(4)
    ]

    for copies in (encs, decs, tids, tacts):
        for copy in copies:
            copy.start()
    far_encs[0].start()

    def put_source(j, h, v):
        per = share // LANES
        src_out[h // per, (h % per) * LANES:(h % per + 1) * LANES, j * rows:(j + 1) * rows] = v.T.astype(BF16)

    build_dense(sid_ref, sact_ref, lo_s, key_s, act_s, tmp, put_source, high)
    for copy in srcs:
        copy.start()

    enc_own[0] = enc_ref[...]
    dec_g[0] = dec_ref[place]

    def put_target(k):
        def put(j, h, v):
            tgt_own[k, j * rows:(j + 1) * rows, h * LANES:(h + 1) * LANES] = v.astype(BF16)

        return put

    tile = 256

    def co_add(i, k, target):
        source = src_out[place] if k == 0 else src_g[k - 1]

        @pl.loop(0, count // tile)
        def _(n):
            at = pl.ds(pl.multiple_of(n * tile, tile), tile)
            term = jnp.dot(source, target[k, :, at], preferred_element_type=F32)
            if k == 0:
                part[i, :, at] = term
            else:
                part[i, :, at] += term

    def virt(i, encoder):
        depth = QUAD * enc_ref.shape[0]
        decoder = dec_g[:, i].reshape(depth, share)
        decoder = decoder.astype(F32).T.astype(BF16)

        @pl.loop(0, count // tile)
        def _(n):
            at = pl.ds(pl.multiple_of(n * tile, tile), tile)
            part[2 + i, :, at] = jnp.dot(
                decoder, encoder[:, :, at].reshape(depth, tile), preferred_element_type=F32
            )

    build_dense(tid_ref, tact_ref, lo_s, key_s, act_s, tmp, put_target(0), high)
    far_tgts[0].start()
    co_add(0, 0, tgt_own)

    for k in range(1, QUAD):
        encs[k - 1].wait_recv()
        far_encs[k].start()
    for copy in decs:
        copy.wait_recv()
    virt(0, enc_own)
    for copy in sums[2]:
        copy.start()
    for copy in far_encs:
        copy.wait_recv()
    virt(1, enc_far)
    for copy in sums[3]:
        copy.start()

    for k in range(1, QUAD):
        tids[k - 1].wait_recv()
        tacts[k - 1].wait_recv()
        build_dense(tid_g.at[k - 1], tact_g.at[k - 1], lo_s, key_s, act_s, tmp, put_target(k), high)
        far_tgts[k].start()
        srcs[k - 1].wait_recv()
        co_add(0, k, tgt_own)
    for copy in sums[0]:
        copy.start()
    for k in range(QUAD):
        far_tgts[k].wait_recv()
        co_add(1, k, tgt_far)
    for copy in sums[1]:
        copy.start()

    own = pl.ds(pl.multiple_of(group * block, block), block)

    def total(i):
        value = part[i, own, :]
        for s in range(1, groups):
            sums[i][s - 1].wait_recv()
            value = value + arrived[s - 1, i]
        return value

    for i, slot in ((0, layer), (1, 1 - layer)):
        out_ref[slot] = total(2 + i) * (total(i) * factor)

    for copies in (tids, tacts, decs, encs, srcs, far_encs, far_tgts, *sums):
        for copy in copies:
            copy.wait_send()


def on_device(src_ids, src_acts, tgt_ids, tgt_acts, enc_cols, dec_rows):
    layer = lax.axis_index("layer")
    shards = lax.axis_size("width")
    groups = shards // QUAD
    count, depth = enc_cols.shape[1:]
    share = count // QUAD
    block = share // groups
    top = src_ids.shape[2] // 2
    tokens = src_ids.shape[1] * 2
    rows, wide = tokens // QUAD, QUAD * top
    factor = (count / top) ** 2 / (tokens * shards)

    def pick(value, index):
        return lax.dynamic_index_in_dim(value, index, 0, False)

    ids = src_ids[0]
    ids = (ids // block % QUAD) * share + ids // (block * QUAD) * block + ids % block
    sid = ids.astype(jnp.int16).reshape(rows, wide)
    sact = src_acts[0].reshape(rows, wide)
    tid = pick(tgt_ids, layer).astype(jnp.int16).reshape(rows, wide)
    tact = pick(tgt_acts, layer).reshape(rows, wide)

    spare = -depth % 16
    enc = jnp.pad(enc_cols[0].T, ((0, spare), (0, 0)))
    dec = dec_rows[0]
    dec = jnp.where(layer == 0, dec, dec[::-1])
    dec = dec.reshape(2, groups, QUAD, block, depth).transpose(2, 0, 4, 1, 3)
    dec = jnp.pad(dec.reshape(QUAD, 2, depth, share), ((0, 0), (0, 0), (0, spare), (0, 0)))
    deep = depth + spare

    def vmem(*shape, kind=BF16):
        return pltpu.VMEM(shape, kind)

    def sems(*shape):
        return [pltpu.SemaphoreType.DMA(shape)] * 2

    out = pl.pallas_call(
        functools.partial(kernel, groups, factor),
        out_shape=jax.ShapeDtypeStruct((2, block, count), F32),
        in_specs=[pl.BlockSpec(memory_space=pltpu.VMEM)] * 6,
        out_specs=pl.BlockSpec(memory_space=pltpu.VMEM),
        scratch_shapes=[
            vmem(QUAD - 1, rows, wide, kind=jnp.int16),
            vmem(QUAD - 1, rows, wide),
            vmem(QUAD, deep, count),
            vmem(QUAD, deep, count),
            vmem(QUAD, 2, deep, share),
            vmem(QUAD, share, tokens),
            vmem(QUAD - 1, share, tokens),
            vmem(QUAD, tokens, count),
            vmem(QUAD, tokens, count),
            vmem(4, share, count, kind=F32),
            vmem(groups - 1, 4, block, count, kind=F32),
            vmem(rows, wide, kind=F32),
            vmem(rows, wide, kind=F32),
            vmem(rows, wide, kind=F32),
            vmem(rows * QUAD * (count // LANES), LANES, kind=F32),
            *sems(QUAD - 1),
            *sems(QUAD - 1),
            *sems(QUAD - 1),
            *sems(QUAD - 1),
            *sems(QUAD - 1),
            *sems(QUAD),
            *sems(QUAD),
            *sems(4, groups - 1),
        ],
        compiler_params=pltpu.CompilerParams(
            collective_id=0, has_side_effects=True, vmem_limit_bytes=56 * 1024 * 1024
        ),
        name="edges",
    )(sid, sact, tid, tact, enc, dec)
    return out[None]


def solution(mesh):
    placed = (
        P("layer", ("parts", "width"), None),
        P("layer", ("parts", "width"), None),
        P(None, ("parts", "width"), None),
        P(None, ("parts", "width"), None),
        P("layer", None, "width"),
        P("layer", None, None, "width"),
    )
    return jax.shard_map(
        on_device,
        mesh=mesh,
        in_specs=placed,
        out_specs=P(("parts", "layer"), None, "width", None),
        check_vma=False,
    )
```

time: 581 us -> 150 us (0.26)
  waiting for transfers between devices: 275 us -> 0 us
  other arithmetic: 188 us -> 2.48 us
  Pallas kernels: 0 us -> 139 us
  local copies, waits for them, and re-layouts: 84.4 us -> 6.66 us
  between operations: 13.6 us -> 0.07 us
  matrix products: 11.3 us -> 0 us
    unnamed x4 -> x0, waiting for transfers between devices: 275 us -> none
    reduce_sum x48 -> x0, other arithmetic: 156 us -> none  [one_block(): return jnp.sum(values, axis=1).astype(jnp.bfloat16)]
    pallas_call x0 -> x1, Pallas kernels: none -> 139 us  [on_device(): pl.pallas_call(functools.partial(kernel, groups, factor), out_shape=jax.S...]
    eq x48 -> x0, local copies, waits for them, and re-layouts: 36.6 us -> none  [one_block(): hits = block_ids[:, :, None] == columns]
    convert_element_type x48 -> x2, other arithmetic: 23.3 us -> 2.19 us  [the longest x1 1.11 us: on_device(): sid = ids.astype(jnp.int16).reshape(rows, wide)]
    unnamed x14 -> x10, local copies, waits for them, and re-layouts: 19.2 us -> 2.74 us
    dot_general x4 -> x0, matrix products: 11.3 us -> none  [the longest x2 6.45 us: co_term(): lax.dot_general(source, target, (((0,), (0,)), ((), ())), preferred_eleme...]
    dynamic_update_slice x48 -> x0, local copies, waits for them, and re-layouts: 11.2 us -> none  [dense_acts(): dense = lax.map(one_block, (id_blocks, act_blocks))]
  transfers between devices with their start and end apart: 3 -> 0, of which waited for: 2 -> 0; matrix products, arithmetic and copies ran while one was open for 49% -> 0% of each run, Pallas kernels for 0% -> 0%
where the time goes in v1:
time: 150 us; the launch traced here: 148 us
  Pallas kernels  139 us (93%)
  local copies, waits for them, and re-layouts  6.66 us (4%)
  other arithmetic  2.48 us (2%)
    pallas_call x1, Pallas kernels, on_device(): pl.pallas_call(functools.partial(kernel, groups, factor), out_shape=jax.S...  139 us

profile of v1, /device:TPU:0, one launch (start us, length us, event | category | flops | bytes accessed | tf_op | source)
XLA Modules:
  0.0 147.7 jit_solution(14295694118555089289)
XLA Ops:
  0.0 0.0 copy-start
  0.0 0.0 copy-start.1
  0.0 1.1 dynamic-slice_convert_fusion
  1.1 0.7 convert_element_type.13.tid_ref
  1.8 0.0 copy-done
  1.8 0.7 reshape.15.tact_ref
  2.5 0.0 copy-done.1
  2.5 0.8 copy.8
  3.3 0.3 reverse_select_fusion
  3.6 0.2 copy.9
  3.8 0.0 copy-start.2
  3.8 0.0 copy-start.3
  3.8 1.6 %copy.10.dec_ref = bf16[4,2,288,256]{3,2,1,0:T(8,128)(2,1)} copy(bf16[4,2,288,256]{2,3,1,0:T(8,128)(2,1)S(1)} %bitcast.10) | data formatting | bytes 2359296 | tf_op jit(solution)/shard_map/reshape | solution.py:239
  5.4 0.0 copy-done.2
  5.4 0.1 squeeze.13
  5.5 1.1 fusion.4.sid_ref
  6.6 0.0 copy-done.3
  6.6 0.7 reshape_squeeze.3.sact_ref
  7.3 138.5 %edges.1 = f32[2,64,1024]{2,1,0:T(8,128)} custom-call(s16[256,256]{1,0:T(8,128)(2,1)} %fusion.4.sid_ref, bf16[256,256]{1,0:T(8,128)(2,1)} %reshape_squeeze.3.sact_ref, s16[256,256]{1,0:T(8,128)(2,1)} %convert_element_type.13.tid_ref, bf16[256,256]{1,0:T(8,128)(2,1)} %reshape.15.tact_ref, bf16[288,1024]{1,0:T(8,128)(2,1)} %bitcast.13, ...), custom_call_target="tpu_custom_call" | custom-call | tf_op jit(solution)/shard_map/edges/pallas_call | solution.py:248
  145.8 1.9 %copy.12 = f32[1,2,64,1024]{3,2,1,0:T(8,128)} copy(f32[1,2,64,1024]{3,2,1,0:T(8,128)} %bitcast.12) | data formatting | bytes 1048576
  (1 shorter events, 0.0 us)
Async XLA Ops:
  0.0 1.8 %copy-start = (bf16[2,512,128]{2,1,0:T(8,128)(2,1)S(1)}, bf16[2,512,128]{2,1,0:T(8,128)(2,1)}, u32[]{:S(2)}) copy-start(bf16[2,512,128]{2,1,0:T(8,128)(2,1)} %param.9) | copy-start | bytes 786436
  0.0 2.5 %copy-start.1 = (bf16[1,2,1024,288]{2,3,1,0:T(8,128)(2,1)S(1)}, bf16[1,2,1024,288]{2,3,1,0:T(8,128)(2,1)}, u32[]{:S(2)}) copy-start(bf16[1,2,1024,288]{2,3,1,0:T(8,128)(2,1)} %param.11) | copy-start | bytes 3538948
  3.8 1.6 %copy-start.2 = (s32[1,512,128]{2,1,0:T(8,128)S(1)}, s32[1,512,128]{2,1,0:T(8,128)}, u32[]{:S(2)}) copy-start(s32[1,512,128]{2,1,0:T(8,128)} %param.6) | copy-start | bytes 786436
  3.8 2.8 %copy-start.3 = (bf16[1,512,128]{2,1,0:T(8,128)(2,1)S(1)}, bf16[1,512,128]{2,1,0:T(8,128)(2,1)}, u32[]{:S(2)}) copy-start(bf16[1,512,128]{2,1,0:T(8,128)(2,1)} %param.7) | copy-start | bytes 393220

commit v2 on v1

--- a/solution.py
+++ b/solution.py
@@ -13,6 +13,8 @@
 QUAD = 4
 LANES = 128
 UNROLL = 16
+TILE = 256
+LEVELS = 32766.0
 
 
 def build_dense(ids_ref, acts_ref, lo_s, key_s, act_s, tmp, put, high):
@@ -57,15 +59,16 @@
     sid_ref, sact_ref, tid_ref, tact_ref, enc_ref, dec_ref,
     out_ref,
     tid_g, tact_g, enc_own, enc_far, dec_g, src_out, src_g, tgt_own, tgt_far,
-    part, arrived, lo_s, key_s, act_s, tmp,
+    part, code, scale, code_in, scale_in, dec_t, lo_s, key_s, act_s, tmp,
     tid_ss, tid_rs, tact_ss, tact_rs, enc_ss, enc_rs, dec_ss, dec_rs, src_ss, src_rs,
-    fe_ss, fe_rs, ft_ss, ft_rs, z_ss, z_rs,
+    fe_ss, fe_rs, ft_ss, ft_rs, code_ss, code_rs, scale_ss, scale_rs,
 ):
     layer = lax.axis_index("layer")
     width = lax.axis_index("width")
     group, place = width // QUAD, width % QUAD
     rows = tid_ref.shape[0]
-    count = enc_ref.shape[1]
+    tiles = enc_ref.shape[0]
+    count = tiles * TILE
     high = count // LANES
     share = count // QUAD
     block = share // groups
@@ -96,35 +99,50 @@
     tids = [remote(tid_ref, tid_g.at[k - 1], tid_ss.at[k - 1], tid_rs.at[k - 1], ids[k]) for k in range(1, QUAD)]
     tacts = [remote(tact_ref, tact_g.at[k - 1], tact_ss.at[k - 1], tact_rs.at[k - 1], ids[k]) for k in range(1, QUAD)]
     decs = [remote(dec_ref.at[peers[k]], dec_g.at[k], dec_ss.at[k - 1], dec_rs.at[k - 1], ids[k]) for k in range(1, QUAD)]
-    encs = [remote(enc_ref, enc_own.at[k], enc_ss.at[k - 1], enc_rs.at[k - 1], ids[k]) for k in range(1, QUAD)]
+    encs = [
+        [remote(enc_ref.at[n], enc_own.at[n, k], enc_ss.at[n, k - 1], enc_rs.at[n, k - 1], ids[k]) for k in range(1, QUAD)]
+        for n in range(tiles)
+    ]
     srcs = [remote(src_out.at[peers[k]], src_g.at[k - 1], src_ss.at[k - 1], src_rs.at[k - 1], ids[k]) for k in range(1, QUAD)]
-    far_encs = [remote(enc_ref if k == 0 else enc_own.at[k], enc_far.at[k], fe_ss.at[k], fe_rs.at[k], pair) for k in range(QUAD)]
+    far_encs = [remote(enc_own.at[n], enc_far.at[n], fe_ss.at[n], fe_rs.at[n], pair) for n in range(tiles)]
     far_tgts = [remote(tgt_own.at[k], tgt_far.at[k], ft_ss.at[k], ft_rs.at[k], pair) for k in range(QUAD)]
-    sums = [
-        [
-            remote(
-                part.at[i, pl.ds(pl.multiple_of(ring[s] * block, block), block), :],
-                arrived.at[s - 1, i], z_ss.at[i, s - 1], z_rs.at[i, s - 1], ring_ids[s],
-            )
-            for s in range(1, groups)
-        ]
-        for i in range(4)
-    ]
-
-    for copies in (encs, decs, tids, tacts):
+    stages = [(slice(0, 1), slice(None)), (slice(1, 2), slice(None))]
+    stages += [(slice(2, 4), slice(n, n + 1)) for n in range(tiles)]
+
+    def stage_copies(c, s):
+        i, n = stages[c]
+        rows_to = pl.ds(pl.multiple_of(ring[s] * block, block), block)
+        return (
+            remote(code.at[i, n, rows_to, :], code_in.at[s - 1, i, n], code_ss.at[c, s - 1], code_rs.at[c, s - 1], ring_ids[s]),
+            remote(scale.at[ring[s], i, n], scale_in.at[s - 1, i, n], scale_ss.at[c, s - 1], scale_rs.at[c, s - 1], ring_ids[s]),
+        )
+
+    sums = [[copy for s in range(1, groups) for copy in stage_copies(c, s)] for c in range(len(stages))]
+
+    for copies in (tids, tacts):
         for copy in copies:
             copy.start()
-    far_encs[0].start()
+
+    def encode(i, n):
+        for g in range(groups):
+            at = pl.ds(g * block, block)
+            value = part[i, n, at, :]
+            size = jnp.abs(value)
+            top = jnp.max(size, axis=0, keepdims=True)
+            inverse = jnp.where(top > 0, 1.0 / top, 0.0)
+            level = (jnp.sqrt(size * inverse) * LEVELS + 0.5).astype(jnp.int32)
+            code[i, n, at, :] = jnp.where(value < 0, -level, level).astype(jnp.int16)
+            scale[g, i, n] = top * (1.0 / LEVELS**2)
 
     def put_source(j, h, v):
         per = share // LANES
         src_out[h // per, (h % per) * LANES:(h % per + 1) * LANES, j * rows:(j + 1) * rows] = v.T.astype(BF16)
 
     build_dense(sid_ref, sact_ref, lo_s, key_s, act_s, tmp, put_source, high)
-    for copy in srcs:
+    for copy in srcs + decs:
         copy.start()
 
-    enc_own[0] = enc_ref[...]
+    enc_own[:, 0] = enc_ref[...]
     dec_g[0] = dec_ref[place]
 
     def put_target(k):
@@ -133,49 +151,35 @@
 
         return put
 
-    tile = 256
-
     def co_add(i, k, target):
         source = src_out[place] if k == 0 else src_g[k - 1]
 
-        @pl.loop(0, count // tile)
+        @pl.loop(0, tiles)
         def _(n):
-            at = pl.ds(pl.multiple_of(n * tile, tile), tile)
+            at = pl.ds(pl.multiple_of(n * TILE, TILE), TILE)
             term = jnp.dot(source, target[k, :, at], preferred_element_type=F32)
             if k == 0:
-                part[i, :, at] = term
+                part[i, n] = term
             else:
-                part[i, :, at] += term
-
-    def virt(i, encoder):
-        depth = QUAD * enc_ref.shape[0]
-        decoder = dec_g[:, i].reshape(depth, share)
-        decoder = decoder.astype(F32).T.astype(BF16)
-
-        @pl.loop(0, count // tile)
-        def _(n):
-            at = pl.ds(pl.multiple_of(n * tile, tile), tile)
-            part[2 + i, :, at] = jnp.dot(
-                decoder, encoder[:, :, at].reshape(depth, tile), preferred_element_type=F32
-            )
+                part[i, n] += term
+            if k == QUAD - 1:
+                encode(i, n)
+
+    depth = QUAD * enc_ref.shape[1]
+
+    def virt(i, n, encoder):
+        part[2 + i, n] = jnp.dot(
+            dec_t[i], encoder[n].reshape(depth, TILE), preferred_element_type=F32
+        )
+        encode(2 + i, n)
 
     build_dense(tid_ref, tact_ref, lo_s, key_s, act_s, tmp, put_target(0), high)
     far_tgts[0].start()
     co_add(0, 0, tgt_own)
 
-    for k in range(1, QUAD):
-        encs[k - 1].wait_recv()
-        far_encs[k].start()
-    for copy in decs:
-        copy.wait_recv()
-    virt(0, enc_own)
-    for copy in sums[2]:
-        copy.start()
-    for copy in far_encs:
-        copy.wait_recv()
-    virt(1, enc_far)
-    for copy in sums[3]:
-        copy.start()
+    for copies in encs:
+        for copy in copies:
+            copy.start()
 
     for k in range(1, QUAD):
         tids[k - 1].wait_recv()
@@ -192,19 +196,39 @@
     for copy in sums[1]:
         copy.start()
 
+    for copy in decs:
+        copy.wait_recv()
+    for i in range(2):
+        dec_t[i] = dec_g[:, i].reshape(depth, share).astype(F32).T.astype(BF16)
+    for n in range(tiles):
+        for copy in encs[n]:
+            copy.wait_recv()
+        far_encs[n].start()
+        virt(0, n, enc_own)
+        far_encs[n].wait_recv()
+        virt(1, n, enc_far)
+        for copy in sums[2 + n]:
+            copy.start()
+
     own = pl.ds(pl.multiple_of(group * block, block), block)
 
-    def total(i):
-        value = part[i, own, :]
-        for s in range(1, groups):
-            sums[i][s - 1].wait_recv()
-            value = value + arrived[s - 1, i]
+    def total(i, n):
+        value = part[i, n, own, :]
+        for s in range(groups - 1):
+            level = code_in[s, i, n].astype(jnp.int32).astype(F32)
+            value = value + level * jnp.abs(level) * scale_in[s, i, n]
         return value
 
-    for i, slot in ((0, layer), (1, 1 - layer)):
-        out_ref[slot] = total(2 + i) * (total(i) * factor)
-
-    for copies in (tids, tacts, decs, encs, srcs, far_encs, far_tgts, *sums):
+    for c in range(2):
+        for copy in sums[c]:
+            copy.wait_recv()
+    for n in range(tiles):
+        for copy in sums[2 + n]:
+            copy.wait_recv()
+        for i, slot in ((0, layer), (1, 1 - layer)):
+            out_ref[slot, :, n * TILE:(n + 1) * TILE] = total(2 + i, n) * (total(i, n) * factor)
+
+    for copies in (tids, tacts, decs, *encs, srcs, far_encs, far_tgts, *sums):
         for copy in copies:
             copy.wait_send()
 
@@ -238,6 +262,8 @@
     dec = dec.reshape(2, groups, QUAD, block, depth).transpose(2, 0, 4, 1, 3)
     dec = jnp.pad(dec.reshape(QUAD, 2, depth, share), ((0, 0), (0, 0), (0, spare), (0, 0)))
     deep = depth + spare
+    tiles = count // TILE
+    enc = enc.reshape(deep, tiles, TILE).transpose(1, 0, 2)
 
     def vmem(*shape, kind=BF16):
         return pltpu.VMEM(shape, kind)
@@ -253,27 +279,32 @@
         scratch_shapes=[
             vmem(QUAD - 1, rows, wide, kind=jnp.int16),
             vmem(QUAD - 1, rows, wide),
-            vmem(QUAD, deep, count),
-            vmem(QUAD, deep, count),
+            vmem(tiles, QUAD, deep, TILE),
+            vmem(tiles, QUAD, deep, TILE),
             vmem(QUAD, 2, deep, share),
             vmem(QUAD, share, tokens),
             vmem(QUAD - 1, share, tokens),
             vmem(QUAD, tokens, count),
             vmem(QUAD, tokens, count),
-            vmem(4, share, count, kind=F32),
-            vmem(groups - 1, 4, block, count, kind=F32),
+            vmem(4, tiles, share, TILE, kind=F32),
+            vmem(4, tiles, share, TILE, kind=jnp.int16),
+            vmem(groups, 4, tiles, 1, TILE, kind=F32),
+            vmem(groups - 1, 4, tiles, block, TILE, kind=jnp.int16),
+            vmem(groups - 1, 4, tiles, 1, TILE, kind=F32),
+            vmem(2, share, QUAD * deep),
             vmem(rows, wide, kind=F32),
             vmem(rows, wide, kind=F32),
             vmem(rows, wide, kind=F32),
             vmem(rows * QUAD * (count // LANES), LANES, kind=F32),
             *sems(QUAD - 1),
             *sems(QUAD - 1),
+            *sems(tiles, QUAD - 1),
             *sems(QUAD - 1),
             *sems(QUAD - 1),
-            *sems(QUAD - 1),
+            *sems(tiles),
             *sems(QUAD),
-            *sems(QUAD),
-            *sems(4, groups - 1),
+            *sems(2 + tiles, groups - 1),
+            *sems(2 + tiles, groups - 1),
         ],
         compiler_params=pltpu.CompilerParams(
             collective_id=0, has_side_effects=True, vmem_limit_bytes=56 * 1024 * 1024

time: 150 us -> 129 us (0.86); the launches traced: 148 us -> 129 us
  Pallas kernels: 139 us -> 119 us
    pallas_call x1, Pallas kernels: 139 us -> 119 us  [on_device(): pl.pallas_call(functools.partial(kernel, groups, factor), out_shape=jax.S...]
where the time goes in v2:
time: 129 us
  Pallas kernels  119 us (92%)
  local copies, waits for them, and re-layouts  7.57 us (6%)
  other arithmetic  2.48 us (2%)
    pallas_call x1, Pallas kernels, on_device(): pl.pallas_call(functools.partial(kernel, groups, factor), out_shape=jax.S...  119 us
    unnamed x12, local copies, waits for them, and re-layouts  2.74 us

profile of v2, /device:TPU:0, one launch (start us, length us, event | category | flops | bytes accessed | tf_op | source)
XLA Modules:
  0.0 128.8 jit_solution(1543462400855524536)
XLA Ops:
  0.0 0.0 copy-start
  0.0 0.0 copy-start.1
  0.0 1.1 dynamic-slice_convert_fusion
  1.1 0.7 convert_element_type.13.tid_ref
  1.8 0.0 copy-done
  1.8 0.7 reshape.18.tact_ref
  2.5 0.0 copy-done.1
  2.5 0.8 copy.9
  3.4 0.3 reverse_select_fusion
  3.6 0.2 copy.10
  3.8 0.0 copy-start.2
  3.8 0.0 copy-start.3
  3.9 1.6 %copy.11.dec_ref = bf16[4,2,288,256]{3,2,1,0:T(8,128)(2,1)} copy(bf16[4,2,288,256]{2,3,1,0:T(8,128)(2,1)S(1)} %bitcast.17) | data formatting | bytes 2359296 | tf_op jit(solution)/shard_map/reshape | solution.py:263
  5.4 0.0 copy-start.4
  5.4 0.0 copy-done.2
  5.4 0.9 copy.14
  6.3 0.0 copy-done.3
  6.3 0.1 squeeze.13
  6.4 1.1 fusion.4.sid_ref
  7.5 0.0 copy-done.4
  7.5 0.7 reshape_squeeze.3.sact_ref
  8.2 118.6 %edges.1 = f32[2,64,1024]{2,1,0:T(8,128)} custom-call(s16[256,256]{1,0:T(8,128)(2,1)} %fusion.4.sid_ref, bf16[256,256]{1,0:T(8,128)(2,1)} %reshape_squeeze.3.sact_ref, s16[256,256]{1,0:T(8,128)(2,1)} %convert_element_type.13.tid_ref, bf16[256,256]{1,0:T(8,128)(2,1)} %reshape.18.tact_ref, bf16[4,288,256]{2,1,0:T(8,128)(2,1)} %bitcast.19, ...), custom_call_target="tpu_custom_call" | custom-call | tf_op jit(solution)/shard_map/edges/pallas_call | solution.py:274
  126.9 1.9 %copy.16 = f32[1,2,64,1024]{3,2,1,0:T(8,128)} copy(f32[1,2,64,1024]{3,2,1,0:T(8,128)} %bitcast.20) | data formatting | bytes 1048576
  (1 shorter events, 0.0 us)
Async XLA Ops:
  0.0 1.8 %copy-start = (bf16[2,512,128]{2,1,0:T(8,128)(2,1)S(1)}, bf16[2,512,128]{2,1,0:T(8,128)(2,1)}, u32[]{:S(2)}) copy-start(bf16[2,512,128]{2,1,0:T(8,128)(2,1)} %param.9) | copy-start | bytes 786436
  0.0 2.5 %copy-start.1 = (bf16[1,2,1024,288]{2,3,1,0:T(8,128)(2,1)S(1)}, bf16[1,2,1024,288]{2,3,1,0:T(8,128)(2,1)}, u32[]{:S(2)}) copy-start(bf16[1,2,1024,288]{2,3,1,0:T(8,128)(2,1)} %param.11) | copy-start | bytes 3538948
  3.8 1.6 %copy-start.2 = (bf16[1,1024,288]{1,2,0:T(8,128)(2,1)S(1)}, bf16[1,1024,288]{1,2,0:T(8,128)(2,1)}, u32[]{:S(2)}) copy-start(bf16[1,1024,288]{1,2,0:T(8,128)(2,1)} %param.10) | copy-start | bytes 1769476
  3.8 2.5 %copy-start.3 = (s32[1,512,128]{2,1,0:T(8,128)S(1)}, s32[1,512,128]{2,1,0:T(8,128)}, u32[]{:S(2)}) copy-start(s32[1,512,128]{2,1,0:T(8,128)} %param.6) | copy-start | bytes 786436
  5.4 2.1 %copy-start.4 = (bf16[1,512,128]{2,1,0:T(8,128)(2,1)S(1)}, bf16[1,512,128]{2,1,0:T(8,128)(2,1)}, u32[]{:S(2)}) copy-start(bf16[1,512,128]{2,1,0:T(8,128)(2,1)} %param.7) | copy-start | bytes 393220

commit v3 on v2

--- a/solution.py
+++ b/solution.py
@@ -12,7 +12,7 @@
 BF16 = jnp.bfloat16
 QUAD = 4
 LANES = 128
-UNROLL = 16
+UNROLL = 32
 TILE = 256
 LEVELS = 32766.0
 
@@ -20,6 +20,7 @@
 def build_dense(ids_ref, acts_ref, lo_s, key_s, act_s, tmp, put, high):
     rows, wide = ids_ref.shape
     per = QUAD * high
+    step = per + 8
     ids = ids_ref[...].astype(jnp.int32)
     token = lax.broadcasted_iota(jnp.int32, ids.shape, 1) // (wide // QUAD)
     lo_s[...] = (ids % LANES).astype(F32)
@@ -41,7 +42,7 @@
             [jnp.where(key == (sub + 16 * i).astype(BF16), act, zero) for i in range(per // 16)], 0
         )
         out = lax.dot_general(a, b, (((1,), (1,)), ((), ())), preferred_element_type=F32)
-        tmp[pl.ds(pl.multiple_of(r * per, per), per), :] = out
+        tmp[pl.ds(pl.multiple_of(r * step, 8), per), :] = out
 
     def many(g, carry):
         for i in range(UNROLL):
@@ -51,7 +52,7 @@
     lax.fori_loop(0, rows // UNROLL, many, 0)
     for j in range(QUAD):
         for h in range(high):
-            put(j, h, tmp[pl.ds(j * high + h, rows, stride=per), :])
+            put(j, h, tmp[pl.ds(j * high + h, rows, stride=step), :])
 
 
 def kernel(
@@ -119,7 +120,7 @@
 
     sums = [[copy for s in range(1, groups) for copy in stage_copies(c, s)] for c in range(len(stages))]
 
-    for copies in (tids, tacts):
+    for copies in (tids, tacts, decs, *encs):
         for copy in copies:
             copy.start()
 
@@ -139,7 +140,7 @@
         src_out[h // per, (h % per) * LANES:(h % per + 1) * LANES, j * rows:(j + 1) * rows] = v.T.astype(BF16)
 
     build_dense(sid_ref, sact_ref, lo_s, key_s, act_s, tmp, put_source, high)
-    for copy in srcs + decs:
+    for copy in srcs:
         copy.start()
 
     enc_own[:, 0] = enc_ref[...]
@@ -177,25 +178,14 @@
     far_tgts[0].start()
     co_add(0, 0, tgt_own)
 
-    for copies in encs:
-        for copy in copies:
-            copy.start()
-
-    for k in range(1, QUAD):
+    def target_of(k):
         tids[k - 1].wait_recv()
         tacts[k - 1].wait_recv()
         build_dense(tid_g.at[k - 1], tact_g.at[k - 1], lo_s, key_s, act_s, tmp, put_target(k), high)
         far_tgts[k].start()
-        srcs[k - 1].wait_recv()
-        co_add(0, k, tgt_own)
-    for copy in sums[0]:
-        copy.start()
-    for k in range(QUAD):
-        far_tgts[k].wait_recv()
-        co_add(1, k, tgt_far)
-    for copy in sums[1]:
-        copy.start()
-
+
+    target_of(1)
+    target_of(2)
     for copy in decs:
         copy.wait_recv()
     for i in range(2):
@@ -209,6 +199,18 @@
         virt(1, n, enc_far)
         for copy in sums[2 + n]:
             copy.start()
+
+    target_of(3)
+    for k in range(1, QUAD):
+        srcs[k - 1].wait_recv()
+        co_add(0, k, tgt_own)
+    for copy in sums[0]:
+        copy.start()
+    for k in range(QUAD):
+        far_tgts[k].wait_recv()
+        co_add(1, k, tgt_far)
+    for copy in sums[1]:
+        copy.start()
 
     own = pl.ds(pl.multiple_of(group * block, block), block)
 
@@ -295,7 +297,7 @@
             vmem(rows, wide, kind=F32),
             vmem(rows, wide, kind=F32),
             vmem(rows, wide, kind=F32),
-            vmem(rows * QUAD * (count // LANES), LANES, kind=F32),
+            vmem(rows * (QUAD * (count // LANES) + 8), LANES, kind=F32),
             *sems(QUAD - 1),
             *sems(QUAD - 1),
             *sems(tiles, QUAD - 1),

time: 129 us -> 118 us (0.915)
  Pallas kernels: 119 us -> 108 us
    pallas_call x1, Pallas kernels: 119 us -> 108 us  [on_device(): pl.pallas_call(functools.partial(kernel, groups, factor), out_shape=jax.S...]
where the time goes in v3:
time: 118 us
  Pallas kernels  108 us (92%)
  local copies, waits for them, and re-layouts  7.57 us (6%)
  other arithmetic  2.48 us (2%)
    pallas_call x1, Pallas kernels, on_device(): pl.pallas_call(functools.partial(kernel, groups, factor), out_shape=jax.S...  108 us
    unnamed x12, local copies, waits for them, and re-layouts  2.74 us

profile of v3, /device:TPU:0, one launch (start us, length us, event | category | flops | bytes accessed | tf_op | source)
XLA Modules:
  0.0 118.1 jit_solution(17508844300706696636)
XLA Ops:
  0.0 0.0 copy-start
  0.0 0.0 copy-start.1
  0.0 1.1 dynamic-slice_convert_fusion
  1.1 0.7 convert_element_type.13.tid_ref
  1.8 0.0 copy-done
  1.8 0.7 reshape.18.tact_ref
  2.5 0.0 copy-done.1
  2.5 0.8 copy.9
  3.4 0.3 reverse_select_fusion
  3.6 0.2 copy.10
  3.8 0.0 copy-start.2
  3.8 0.0 copy-start.3
  3.9 1.6 %copy.11.dec_ref = bf16[4,2,288,256]{3,2,1,0:T(8,128)(2,1)} copy(bf16[4,2,288,256]{2,3,1,0:T(8,128)(2,1)S(1)} %bitcast.17) | data formatting | bytes 2359296 | tf_op jit(solution)/shard_map/reshape | solution.py:265
  5.4 0.0 copy-start.4
  5.4 0.0 copy-done.2
  5.4 0.9 copy.14
  6.3 0.0 copy-done.3
  6.3 0.1 squeeze.13
  6.4 1.1 fusion.4.sid_ref
  7.5 0.0 copy-done.4
  7.5 0.7 reshape_squeeze.3.sact_ref
  8.2 108.0 %edges.1 = f32[2,64,1024]{2,1,0:T(8,128)} custom-call(s16[256,256]{1,0:T(8,128)(2,1)} %fusion.4.sid_ref, bf16[256,256]{1,0:T(8,128)(2,1)} %reshape_squeeze.3.sact_ref, s16[256,256]{1,0:T(8,128)(2,1)} %convert_element_type.13.tid_ref, bf16[256,256]{1,0:T(8,128)(2,1)} %reshape.18.tact_ref, bf16[4,288,256]{2,1,0:T(8,128)(2,1)} %bitcast.19, ...), custom_call_target="tpu_custom_call" | custom-call | tf_op jit(solution)/shard_map/edges/pallas_call | solution.py:276
  116.2 1.9 %copy.16 = f32[1,2,64,1024]{3,2,1,0:T(8,128)} copy(f32[1,2,64,1024]{3,2,1,0:T(8,128)} %bitcast.20) | data formatting | bytes 1048576
  (1 shorter events, 0.0 us)
Async XLA Ops:
  0.0 1.8 %copy-start = (bf16[2,512,128]{2,1,0:T(8,128)(2,1)S(1)}, bf16[2,512,128]{2,1,0:T(8,128)(2,1)}, u32[]{:S(2)}) copy-start(bf16[2,512,128]{2,1,0:T(8,128)(2,1)} %param.9) | copy-start | bytes 786436
  0.0 2.5 %copy-start.1 = (bf16[1,2,1024,288]{2,3,1,0:T(8,128)(2,1)S(1)}, bf16[1,2,1024,288]{2,3,1,0:T(8,128)(2,1)}, u32[]{:S(2)}) copy-start(bf16[1,2,1024,288]{2,3,1,0:T(8,128)(2,1)} %param.11) | copy-start | bytes 3538948
  3.8 1.6 %copy-start.2 = (bf16[1,1024,288]{1,2,0:T(8,128)(2,1)S(1)}, bf16[1,1024,288]{1,2,0:T(8,128)(2,1)}, u32[]{:S(2)}) copy-start(bf16[1,1024,288]{1,2,0:T(8,128)(2,1)} %param.10) | copy-start | bytes 1769476
  3.8 2.5 %copy-start.3 = (s32[1,512,128]{2,1,0:T(8,128)S(1)}, s32[1,512,128]{2,1,0:T(8,128)}, u32[]{:S(2)}) copy-start(s32[1,512,128]{2,1,0:T(8,128)} %param.6) | copy-start | bytes 786436
  5.4 2.1 %copy-start.4 = (bf16[1,512,128]{2,1,0:T(8,128)(2,1)S(1)}, bf16[1,512,128]{2,1,0:T(8,128)(2,1)}, u32[]{:S(2)}) copy-start(bf16[1,512,128]{2,1,0:T(8,128)(2,1)} %param.7) | copy-start | bytes 393220

commit v4 on v3

--- a/solution.py
+++ b/solution.py
@@ -120,7 +120,8 @@
 
     sums = [[copy for s in range(1, groups) for copy in stage_copies(c, s)] for c in range(len(stages))]
 
-    for copies in (tids, tacts, decs, *encs):
+    early = tiles // 2
+    for copies in (tids, tacts, decs, *encs[:early]):
         for copy in copies:
             copy.start()
 
@@ -140,8 +141,9 @@
         src_out[h // per, (h % per) * LANES:(h % per + 1) * LANES, j * rows:(j + 1) * rows] = v.T.astype(BF16)
 
     build_dense(sid_ref, sact_ref, lo_s, key_s, act_s, tmp, put_source, high)
-    for copy in srcs:
-        copy.start()
+    for copies in (srcs, *encs[early:]):
+        for copy in copies:
+            copy.start()
 
     enc_own[:, 0] = enc_ref[...]
     dec_g[0] = dec_ref[place]
@@ -190,7 +192,7 @@
         copy.wait_recv()
     for i in range(2):
         dec_t[i] = dec_g[:, i].reshape(depth, share).astype(F32).T.astype(BF16)
-    for n in range(tiles):
+    for n in range(early):
         for copy in encs[n]:
             copy.wait_recv()
         far_encs[n].start()
@@ -211,6 +213,17 @@
         co_add(1, k, tgt_far)
     for copy in sums[1]:
         copy.start()
+
+    for n in range(early, tiles):
+        for copy in encs[n]:
+            copy.wait_recv()
+        far_encs[n].start()
+        virt(0, n, enc_own)
+        far_encs[n].wait_recv()
+        virt(1, n, enc_far)
+        for copy in sums[2 + n]:
+            copy.start()
+
 
     own = pl.ds(pl.multiple_of(group * block, block), block)
 

time: 118 us -> 118 us (level)
  no operation moved by 1% of the time
where the time goes in v4:
time: 118 us; the launch traced here: 117 us
  Pallas kernels  107 us (91%)
  local copies, waits for them, and re-layouts  7.57 us (6%)
  other arithmetic  2.48 us (2%)
    pallas_call x1, Pallas kernels, on_device(): pl.pallas_call(functools.partial(kernel, groups, factor), out_shape=jax.S...  107 us
    unnamed x12, local copies, waits for them, and re-layouts  2.74 us

profile of v4, /device:TPU:0, one launch (start us, length us, event | category | flops | bytes accessed | tf_op | source)
XLA Modules:
  0.0 117.5 jit_solution(8366634252843876234)
XLA Ops:
  0.0 0.0 copy-start
  0.0 0.0 copy-start.1
  0.0 1.1 dynamic-slice_convert_fusion
  1.1 0.7 convert_element_type.13.tid_ref
  1.8 0.0 copy-done
  1.8 0.7 reshape.18.tact_ref
  2.5 0.0 copy-done.1
  2.5 0.8 copy.9
  3.4 0.3 reverse_select_fusion
  3.6 0.2 copy.10
  3.8 0.0 copy-start.2
  3.8 0.0 copy-start.3
  3.9 1.6 %copy.11.dec_ref = bf16[4,2,288,256]{3,2,1,0:T(8,128)(2,1)} copy(bf16[4,2,288,256]{2,3,1,0:T(8,128)(2,1)S(1)} %bitcast.17) | data formatting | bytes 2359296 | tf_op jit(solution)/shard_map/reshape | solution.py:278
  5.4 0.0 copy-start.4
  5.4 0.0 copy-done.2
  5.4 0.9 copy.14
  6.3 0.0 copy-done.3
  6.3 0.1 squeeze.13
  6.4 1.1 fusion.4.sid_ref
  7.5 0.0 copy-done.4
  7.5 0.7 reshape_squeeze.3.sact_ref
  8.2 107.4 %edges.1 = f32[2,64,1024]{2,1,0:T(8,128)} custom-call(s16[256,256]{1,0:T(8,128)(2,1)} %fusion.4.sid_ref, bf16[256,256]{1,0:T(8,128)(2,1)} %reshape_squeeze.3.sact_ref, s16[256,256]{1,0:T(8,128)(2,1)} %convert_element_type.13.tid_ref, bf16[256,256]{1,0:T(8,128)(2,1)} %reshape.18.tact_ref, bf16[4,288,256]{2,1,0:T(8,128)(2,1)} %bitcast.19, ...), custom_call_target="tpu_custom_call" | custom-call | tf_op jit(solution)/shard_map/edges/pallas_call | solution.py:289
  115.6 1.9 %copy.16 = f32[1,2,64,1024]{3,2,1,0:T(8,128)} copy(f32[1,2,64,1024]{3,2,1,0:T(8,128)} %bitcast.20) | data formatting | bytes 1048576
  (1 shorter events, 0.0 us)
Async XLA Ops:
  0.0 1.8 %copy-start = (bf16[2,512,128]{2,1,0:T(8,128)(2,1)S(1)}, bf16[2,512,128]{2,1,0:T(8,128)(2,1)}, u32[]{:S(2)}) copy-start(bf16[2,512,128]{2,1,0:T(8,128)(2,1)} %param.9) | copy-start | bytes 786436
  0.0 2.5 %copy-start.1 = (bf16[1,2,1024,288]{2,3,1,0:T(8,128)(2,1)S(1)}, bf16[1,2,1024,288]{2,3,1,0:T(8,128)(2,1)}, u32[]{:S(2)}) copy-start(bf16[1,2,1024,288]{2,3,1,0:T(8,128)(2,1)} %param.11) | copy-start | bytes 3538948
  3.8 1.6 %copy-start.2 = (bf16[1,1024,288]{1,2,0:T(8,128)(2,1)S(1)}, bf16[1,1024,288]{1,2,0:T(8,128)(2,1)}, u32[]{:S(2)}) copy-start(bf16[1,1024,288]{1,2,0:T(8,128)(2,1)} %param.10) | copy-start | bytes 1769476
  3.8 2.5 %copy-start.3 = (s32[1,512,128]{2,1,0:T(8,128)S(1)}, s32[1,512,128]{2,1,0:T(8,128)}, u32[]{:S(2)}) copy-start(s32[1,512,128]{2,1,0:T(8,128)} %param.6) | copy-start | bytes 786436
  5.4 2.1 %copy-start.4 = (bf16[1,512,128]{2,1,0:T(8,128)(2,1)S(1)}, bf16[1,512,128]{2,1,0:T(8,128)(2,1)}, u32[]{:S(2)}) copy-start(bf16[1,512,128]{2,1,0:T(8,128)(2,1)} %param.7) | copy-start | bytes 393220
